TPU v7x, 256 devices: a whole 4x4x8 slice. The times are simulated.
256 devices in a mesh: noise: 8 (over z), row: 16 (over y, x), col: 2 (over core).
Axes of the slice: x: 4, y: 4, z: 8, core: 2. Of those that a mesh axis runs over, the one named last changes fastest.
Arguments:
- images: bfloat16 [256, 4, 6144], P('row', None, 'col'), may hold values from -40 to 40
- gain: float32 [6144], P('col'), may hold values from 0.3 to 3.5
- up_weight: bfloat16 [6144, 12288], P('col', 'row'), may hold values from -0.078125 to 0.078125
- down_weight: bfloat16 [12288, 6144], P('row', 'col'), may hold values from -0.0546875 to 0.0546875
- cotangent: bfloat16 [256, 16, 6144], P('row', 'noise', 'col'), may hold values from -6 to 6
- seeds: int32 [16], P('noise'), may hold values from 0 to 999999
- assign: int32 [16, 1], replicated, may hold values from 0 to 3, as said below
Outputs:
- saliency: float32 [256, 4, 6144], P('row', None, 'col')
Inputs may be any that keep to these rules, and one draw needn't show every extreme that they name: `assign`: every one of the 4 images is named by at least one copy.
All inputs are finite; a program needn't handle non-finite values.
Results may differ from a plain program's by a relative error of at most 0.0019.
Values may be sent and summed in bfloat16 or wider, within the bound.
A program may use at most 64 MiB of HBM per device.

v0:
```python
import math
import jax
import jax.numpy as jnp
from jax import lax
from jax.sharding import PartitionSpec as P

D = 6144
noise_scale = 0.6
gelu_coef = 0.044715
root_term = math.sqrt(2.0 / math.pi)


def mix_noise(seed_value, token_index, feature_index, width):
    linear = token_index[:, None] * width + feature_index[None, :]
    mixed = linear * 1664525 + seed_value * 1013904223
    mixed = mixed ^ mixed >> 13
    mixed = mixed * 1274126177
    mixed = mixed ^ mixed >> 16
    return ((mixed & 65535).astype(jnp.float32) - 32767.5) * (1.0 / 18918.0)


def gelu_slope(preact):
    inner = root_term * (preact + gelu_coef * preact * preact * preact)
    tanh_val = jnp.tanh(inner)
    return 0.5 * (1.0 + tanh_val) + 0.5 * preact * (1.0 - tanh_val * tanh_val) * root_term * (
        1.0 + 3.0 * gelu_coef * preact * preact
    )


def body(images, gain, up_weight, down_weight, cotangent, seeds, assign):
    slot_count = seeds.shape[0]
    tok_local = images.shape[0]
    image_count = images.shape[1]
    width_local = images.shape[2]
    col_index = lax.axis_index("col")
    row_index = lax.axis_index("row")
    noise_index = lax.axis_index("noise")
    image_ids = jnp.arange(image_count, dtype=jnp.int32)
    my_images = lax.dynamic_slice_in_dim(assign[:, 0], noise_index * slot_count, slot_count)
    onehot = (my_images[:, None] == image_ids[None, :]).astype(jnp.float32)
    clean_rows = jnp.einsum(
        "si,tid->tsd", onehot.astype(jnp.bfloat16), images, preferred_element_type=jnp.float32
    )
    token_index = row_index * tok_local + jnp.arange(tok_local, dtype=jnp.int32)
    feature_index = col_index * width_local + jnp.arange(width_local, dtype=jnp.int32)
    noise_field = jax.vmap(
        lambda seed_value: mix_noise(seed_value, token_index, feature_index, D), out_axes=1
    )(seeds)
    noisy_rows = clean_rows + noise_scale * noise_field
    feat_mean = lax.psum(jnp.sum(noisy_rows, axis=-1), "col") / D
    centred = noisy_rows - feat_mean[..., None]
    feat_var = lax.psum(jnp.sum(centred * centred, axis=-1), "col") / D
    inv_std = lax.rsqrt(feat_var + 1e-06)[..., None]
    normed = centred * inv_std
    scaled = (normed * gain).astype(jnp.bfloat16)
    gathered = (
        lax.all_gather(scaled, "row", axis=0, tiled=True),
        lax.all_gather(cotangent, "row", axis=0, tiled=True),
    )
    row_count = gathered[0].shape[0] * slot_count
    full_scaled = gathered[0].reshape(row_count, width_local)
    full_cotangent = gathered[1].reshape(row_count, width_local)
    preact_part = jnp.dot(full_scaled, up_weight, preferred_element_type=jnp.float32)
    back_part = jnp.einsum(
        "td,hd->th", full_cotangent, down_weight, preferred_element_type=jnp.float32
    )
    preact, back_grad = lax.psum((preact_part, back_part), "col")
    hidden_grad = (back_grad * gelu_slope(preact)).astype(jnp.bfloat16)
    scaled_grad = lax.psum_scatter(
        jnp.einsum("th,dh->td", hidden_grad, up_weight, preferred_element_type=jnp.float32),
        "row",
        scatter_dimension=0,
        tiled=True,
    )
    scaled_grad = scaled_grad.reshape(tok_local, slot_count, width_local)
    normed_grad = scaled_grad * gain
    grad_sum, grad_dot = lax.psum(
        (jnp.sum(normed_grad, axis=-1), jnp.sum(normed_grad * normed, axis=-1)), "col"
    )
    input_grad = cotangent.astype(jnp.float32) + inv_std * (
        normed_grad - grad_sum[..., None] / D - normed * (grad_dot[..., None] / D)
    )
    partial_totals = jnp.einsum("si,tsd->tid", onehot, input_grad, precision=lax.Precision.HIGHEST)
    onehot_all = (assign[:, 0][:, None] == image_ids[None, :]).astype(jnp.float32)
    counts = jnp.sum(onehot_all, axis=0)
    totals = lax.psum(partial_totals, "noise")
    return totals / counts[None, :, None]


def solution(mesh):
    placed = (
        P("row", None, "col"),
        P("col"),
        P("col", "row"),
        P("row", "col"),
        P("row", "noise", "col"),
        P("noise"),
        P(),
    )
    return jax.shard_map(
        body, mesh=mesh, in_specs=placed, out_specs=P("row", None, "col"), check_vma=False
    )
```

profile of v0, /device:TPU:2, one launch (start us, length us, event | category | flops | bytes accessed | tf_op | source)
XLA Modules:
  0.0 361.4 jit_solution(3402559265118721403)
XLA Ops:
  6.5 0.0 copy-start
  6.5 0.0 all-gather.5.cloned.1.call-start
  6.6 0.7 broadcast_multiply_fusion.3
  7.3 0.7 dynamic-slice_bitcast_fusion
  8.0 0.1 add_multiply_fusion
  8.1 0.0 copy-done
  8.1 0.0 copy-start.3
  8.1 0.9 fusion.41
  9.0 2.5 psum.49
  11.5 0.4 multiply_reduce_fusion.2
  11.8 2.5 psum.50
  14.3 0.0 copy-done.3
  14.3 1.0 multiply_convert_fusion
  15.3 0.0 all-gather.5.cloned.1.call-update
  15.3 0.0 all-gather.3.cloned.1.call-start
  15.4 0.7 all-gather.3.cloned.1.call-update
  16.1 0.0 all-reduce.7.cloned.1.call-start
  16.1 54.5 %all-gather.5.cloned.1.call-done = bf16[256,2,3072]{2,1,0:T(2,128)(2,1)} async-done(((bf16[16,2,3072]{2,1,0:T(2,128)(2,1)}), bf16[256,2,3072]{2,1,0:T(2,128)(2,1)}) %all-gather.5.cloned.1.call-update) | async-done | bytes 3145744 | tf_op jit(solution)/shard_map/all_gather | solution.py:57
  70.6 7.5 %reshape.60 = bf16[512,3072]{1,0:T(8,128)(2,1)} reshape(bf16[256,2,3072]{2,1,0:T(2,128)(2,1)} %all-gather.5.cloned.1.call-done) | data formatting | bytes 6291456 | tf_op jit(solution)/shard_map/reshape | solution.py:61
  78.2 7.1 %fusion.43 = f32[512,768]{1,0:T(8,128)} fusion(bf16[512,3072]{1,0:T(8,128)(2,1)} %reshape.60, bf16[3072,768]{1,0:T(8,128)(2,1)} %param.9), kind=kOutput, calls=%fused_computation.66 | convolution fusion | flops 2415919104 | bytes 9437184 | tf_op jit(solution)/shard_map/dot_general | solution.py:63
  85.2 39.8 %all-gather.3.cloned.1.call-done = bf16[256,2,3072]{2,1,0:T(2,128)(2,1)} async-done(((bf16[16,2,3072]{2,1,0:T(2,128)(2,1)}), bf16[256,2,3072]{2,1,0:T(2,128)(2,1)}) %all-gather.3.cloned.1.call-update) | async-done | bytes 3145744 | tf_op jit(solution)/shard_map/all_gather | solution.py:58
  125.0 7.5 %reshape.59 = bf16[512,3072]{1,0:T(8,128)(2,1)} reshape(bf16[256,2,3072]{2,1,0:T(2,128)(2,1)} %all-gather.3.cloned.1.call-done) | data formatting | bytes 6291456 | tf_op jit(solution)/shard_map/reshape | solution.py:62
  132.6 7.1 %fusion.42 = f32[512,768]{1,0:T(8,128)} fusion(bf16[512,3072]{1,0:T(8,128)(2,1)} %reshape.59, bf16[768,3072]{1,0:T(8,128)(2,1)} %param.10), kind=kOutput, calls=%fused_computation.65 | convolution fusion | flops 2415919104 | bytes 9437184 | tf_op jit(solution)/shard_map/td,hd->th/dot_general | solution.py:64
  139.6 0.0 all-reduce.7.cloned.1.call-update
  139.7 0.0 reduce-scatter.2.cloned.1.call-start
  139.7 33.9 %all-reduce.7.cloned.1.call-done = (f32[512,768]{1,0:T(8,128)}, f32[512,768]{1,0:T(8,128)}) async-done(((f32[512,768]{1,0:T(8,128)}, f32[512,768]{1,0:T(8,128)}), (f32[512,768]{1,0:T(8,128)}, f32[512,768]{1,0:T(8,128)})) %all-reduce.7.cloned.1.call-update) | async-done | bytes 3145744 | tf_op jit(solution)/shard_map/psum | solution.py:67
  173.6 9.2 %fusion.8 = f32[512,3072]{1,0:T(8,128)} fusion(bf16[3072,768]{1,0:T(8,128)(2,1)} %param.9, f32[512,768]{1,0:T(8,128)} %get-tuple-element.7, f32[512,768]{1,0:T(8,128)} %get-tuple-element.8), kind=kOutput, calls=%fused_computation.12 | convolution fusion | flops 2423390208 | bytes 14155776 | tf_op jit(solution)/shard_map/th,dh->td/dot_general | solution.py:70
  182.8 0.0 reduce-scatter.2.cloned.1.call-update
  182.8 0.0 copy-start.2
  182.8 0.2 all-reduce.5.cloned.1.call-start
  183.1 87.3 %reduce-scatter.2.cloned.1.call-done = f32[32,3072]{1,0:T(8,128)} async-done(((f32[512,3072]{1,0:T(8,128)}), f32[32,3072]{1,0:T(8,128)}) %reduce-scatter.2.cloned.1.call-update) | async-done | bytes 393232 | tf_op jit(solution)/shard_map/reduce_scatter | solution.py:69
  270.3 0.0 copy-start.1
  270.3 1.3 reshape.61
  271.6 0.5 multiply_reduce_fusion
  272.1 0.0 copy-done.1
  272.1 0.2 multiply_reduce_fusion.1
  272.3 0.1 reduce_sum.50
  272.3 3.3 all-reduce
  275.6 0.0 copy-done.2
  275.7 0.0 copy-start.4
  275.7 2.3 convolution_bitcast_fusion
  278.0 0.0 all-reduce.5.cloned.1.call-update
  278.0 0.0 copy-done.4
  278.0 0.1 convert_reduce_fusion
  278.1 74.4 %all-reduce.5.cloned.1.call-done = f32[16,4,3072]{2,1,0:T(4,128)} async-done(((f32[16,4,3072]{2,1,0:T(4,128)}), f32[16,4,3072]{2,1,0:T(4,128)}) %all-reduce.5.cloned.1.call-update) | async-done | bytes 786448 | tf_op jit(solution)/shard_map/psum | solution.py:86
  352.6 2.3 broadcast_divide_fusion
  (5 shorter events, 0.0 us)
Async XLA Ops:
  6.5 1.5 copy-start
  6.5 64.1 %all-gather.5.cloned.1.call-start = ((), (), s32[]{:S(2)}) async-start(), calls=%async_computation.2 | async-start | bytes 3342336 | tf_op jit(solution)/shard_map/all_gather | solution.py:57
  8.1 6.2 %copy-start.3 = (f32[3072]{0:T(1024)S(1)}, f32[3072]{0:T(1024)}, u32[]{:S(2)}) copy-start(f32[3072]{0:T(1024)} %param.8) | copy-start | bytes 36868
  15.3 109.7 %all-gather.3.cloned.1.call-start = ((), (), s32[]{:S(2)}) async-start(), calls=%async_computation.1 | async-start | bytes 3342336 | tf_op jit(solution)/shard_map/all_gather | solution.py:58
  16.1 157.5 %all-reduce.7.cloned.1.call-start = ((), (), s32[]{:S(2)}) async-start(), calls=%async_computation.5 | async-start | bytes 6291456 | tf_op jit(solution)/shard_map/psum | solution.py:67
  139.7 130.7 %reduce-scatter.2.cloned.1.call-start = ((), (), s32[]{:S(2)}) async-start(), calls=%async_computation.3 | async-start | bytes 6684672 | tf_op jit(solution)/shard_map/reduce_scatter | solution.py:69
  182.8 92.8 %copy-start.2 = (bf16[16,2,3072]{2,1,0:T(2,128)(2,1)S(1)}, bf16[16,2,3072]{2,1,0:T(2,128)(2,1)}, u32[]{:S(2)}) copy-start(bf16[16,2,3072]{2,1,0:T(2,128)(2,1)} %param.11) | copy-start | bytes 589828
  182.8 169.7 %all-reduce.5.cloned.1.call-start = ((), (), s32[]{:S(2)}) async-start(), calls=%async_computation.4 | async-start | bytes 1572864 | tf_op jit(solution)/shard_map/psum | solution.py:86
  270.3 1.8 copy-start.1
  275.7 2.4 copy-start.4
Sparse Core Ops, SparseCore 0:
  15.4 55.1 all-gather.4
  73.1 51.9 all-gather.2
  139.8 33.7 all-reduce.6
  182.9 87.3 reduce-scatter.1
  278.1 74.3 all-reduce.4
where the time goes:
time: 362 us; the launch traced here: 361 us
  waiting for transfers between devices  291 us (80%)
  matrix products  26.6 us (7%)
  local copies, waits for them, and re-layouts  17.2 us (5%)
  between operations  13.2 us (4%)
  blocking collectives  8.21 us (2%)
  other arithmetic  5.16 us (1%)
    reduce_scatter x1, waiting for transfers between devices, body(): lax.psum_scatter(jnp.einsum('th,dh->td', hidden_grad, up_weight, preferre...  87.3 us
    psum x1, waiting for transfers between devices, body(): totals = lax.psum(partial_totals, 'noise')  74.4 us
    all_gather x1, waiting for transfers between devices, body(): lax.all_gather(scaled, 'row', axis=0, tiled=True)  54.5 us
    all_gather x1, waiting for transfers between devices, body(): lax.all_gather(cotangent, 'row', axis=0, tiled=True)  39.8 us
    psum x1, waiting for transfers between devices, body(): preact, back_grad = lax.psum((preact_part, back_part), 'col')  33.9 us
    dot_general x1, matrix products, body(): jnp.einsum('th,dh->td', hidden_grad, up_weight, preferred_element_type=jn...  9.19 us
    reshape x1, local copies, waits for them, and re-layouts, body(): full_scaled = gathered[0].reshape(row_count, width_local)  7.54 us
    reshape x1, local copies, waits for them, and re-layouts, body(): full_cotangent = gathered[1].reshape(row_count, width_local)  7.51 us
  transfers between devices with their start and end apart: 5, of which 5 were waited for; matrix products, arithmetic and copies ran while one was open for 4% of the time, Pallas kernels for 0%

commit v1 on v0

--- a/solution.py
+++ b/solution.py
@@ -8,6 +8,24 @@
 noise_scale = 0.6
 gelu_coef = 0.044715
 root_term = math.sqrt(2.0 / math.pi)
+
+
+def collect(value, axis, dim):
+    ways, here, step = (lax.axis_size(axis), lax.axis_index(axis), value.shape[dim])
+    shape = [n * ways if d == dim else n for d, n in enumerate(value.shape)]
+    full = lax.dynamic_update_slice_in_dim(
+        jnp.zeros(shape, value.dtype), value, here * step, axis=dim
+    )
+    going_up = going_down = value
+    for far in range(1, ways // 2 + 1):
+        going_up = lax.ppermute(going_up, axis, [(d, (d + 1) % ways) for d in range(ways)])
+        full = lax.dynamic_update_slice_in_dim(full, going_up, (here - far) % ways * step, axis=dim)
+        if 2 * far < ways:
+            going_down = lax.ppermute(going_down, axis, [(d, (d - 1) % ways) for d in range(ways)])
+            full = lax.dynamic_update_slice_in_dim(
+                full, going_down, (here + far) % ways * step, axis=dim
+            )
+    return full
 
 
 def mix_noise(seed_value, token_index, feature_index, width):
@@ -53,10 +71,7 @@
     inv_std = lax.rsqrt(feat_var + 1e-06)[..., None]
     normed = centred * inv_std
     scaled = (normed * gain).astype(jnp.bfloat16)
-    gathered = (
-        lax.all_gather(scaled, "row", axis=0, tiled=True),
-        lax.all_gather(cotangent, "row", axis=0, tiled=True),
-    )
+    gathered = (collect(scaled, "row", 0), lax.all_gather(cotangent, "row", axis=0, tiled=True))
     row_count = gathered[0].shape[0] * slot_count
     full_scaled = gathered[0].reshape(row_count, width_local)
     full_cotangent = gathered[1].reshape(row_count, width_local)

time: 362 us -> 348 us (0.961)
  waiting for transfers between devices: 291 us -> 241 us
  starting transfers between devices: 0.35 us -> 34.6 us
    all_gather x1 -> x0, waiting for transfers between devices: 54.5 us -> none  [body(): lax.all_gather(scaled, 'row', axis=0, tiled=True)]
    ppermute x0 -> x15, waiting for transfers between devices: none -> 44.2 us  [the longest x8 43.5 us: collect(): lax.ppermute(going_up, axis, [(d, (d + 1) % ways) for d in range(ways)])]
    all_gather x1, waiting for transfers between devices: 39.8 us -> 0.01 us  [body(): lax.all_gather(cotangent, 'row', axis=0, tiled=True)]
    ppermute x0 -> x15, starting transfers between devices: none -> 34.3 us  [the longest x7 31.8 us: collect(): lax.ppermute(going_down, axis, [(d, (d - 1) % ways) for d in range(ways)])]
    reshape x1, local copies, waits for them, and re-layouts: 7.54 us -> 2.72 us  [body(): full_scaled = gathered[0].reshape(row_count, width_local)]
    dynamic_update_slice x0 -> x15, local copies, waits for them, and re-layouts: none -> 4.18 us  [the longest x8 2.15 us: collect(): lax.dynamic_update_slice_in_dim(full, going_up, (here - far) % ways * ste...]
  transfers between devices with their start and end apart: 5 -> 19, of which waited for: 5 -> 12; matrix products, arithmetic and copies ran while one was open for 4% -> 4% of each run, Pallas kernels for 0% -> 0%
where the time goes in v1:
time: 348 us; the launch traced here: 347 us
  waiting for transfers between devices  241 us (69%)
  starting transfers between devices  34.6 us (10%)
  matrix products  25.7 us (7%)
  local copies, waits for them, and re-layouts  16.9 us (5%)
  between operations  13.6 us (4%)
  blocking collectives  8.23 us (2%)
  other arithmetic  6.89 us (2%)
    reduce_scatter x1, waiting for transfers between devices, body(): lax.psum_scatter(jnp.einsum('th,dh->td', hidden_grad, up_weight, preferre...  87.5 us
    psum x1, waiting for transfers between devices, body(): totals = lax.psum(partial_totals, 'noise')  74.5 us
    ppermute x8, waiting for transfers between devices, collect(): lax.ppermute(going_up, axis, [(d, (d + 1) % ways) for d in range(ways)])  43.5 us
    psum x1, waiting for transfers between devices, body(): preact, back_grad = lax.psum((preact_part, back_part), 'col')  35.1 us
    ppermute x7, starting transfers between devices, collect(): lax.ppermute(going_down, axis, [(d, (d - 1) % ways) for d in range(ways)])  31.8 us
    dot_general x1, matrix products, body(): jnp.einsum('th,dh->td', hidden_grad, up_weight, preferred_element_type=jn...  9.23 us
    dot_general x1, matrix products, body(): jnp.dot(full_scaled, up_weight, preferred_element_type=jnp.float32)  7.05 us
  transfers between devices with their start and end apart: 19, of which 12 were waited for; matrix products, arithmetic and copies ran while one was open for 4% of the time, Pallas kernels for 0%

profile of v1, /device:TPU:2, one launch (start us, length us, event | category | flops | bytes accessed | tf_op | source)
XLA Modules:
  0.0 347.2 jit_solution(7968690782528067931)
XLA Ops:
  6.6 0.7 broadcast_multiply_fusion.3
  7.3 0.1 add_multiply_fusion
  7.3 0.7 fusion.34
  8.1 0.9 fusion.42
  9.0 2.5 psum.49
  11.5 0.4 multiply_reduce_fusion.2
  11.8 2.5 psum.50
  14.3 1.6 broadcast_in_dim.2
  16.0 1.7 constant_dynamic-update-slice_fusion.15
  17.7 1.5 collective-permute-start
  19.2 0.8 collective-permute-start.1
  20.0 0.0 all-gather.2.cloned.1.call-update
  20.0 0.0 all-reduce.7.cloned.1.call-start
  20.3 5.2 %collective-permute-done = bf16[16,2,3072]{2,1,0:T(2,128)(2,1)} collective-permute-done((bf16[16,2,3072]{2,1,0:T(2,128)(2,1)}, bf16[16,2,3072]{2,1,0:T(2,128)(2,1)}, u32[]{:S(2)}, u32[]{:S(2)}) %collective-permute-start) | collective-permute-done | bytes 196640 | tf_op jit(solution)/shard_map/ppermute | solution.py:21
  25.5 1.0 collective-permute-start.2
  26.5 4.1 %collective-permute-start.3 = (bf16[16,2,3072]{2,1,0:T(2,128)(2,1)}, bf16[16,2,3072]{2,1,0:T(2,128)(2,1)S(1)}, u32[]{:S(2)}, u32[]{:S(2)}) collective-permute-start(bf16[16,2,3072]{2,1,0:T(2,128)(2,1)} %collective-permute-done.1), channel_id=1, source_target_pairs={{0,30},{2,0},{4,2},{6,4},{8,6},{10,8},{12,10},{14,12},{16,14},{18,... | collective-permute-start | bytes 589832 | tf_op jit(solution)/shard_map/ppermute | solution.py:24
  30.6 1.1 constant_dynamic-update-slice_fusion.14
  31.7 1.1 constant_dynamic-update-slice_fusion.13
  32.8 2.5 collective-permute-done.2
  35.2 5.5 %collective-permute-start.5 = (bf16[16,2,3072]{2,1,0:T(2,128)(2,1)S(1)}, bf16[16,2,3072]{2,1,0:T(2,128)(2,1)S(1)}, u32[]{:S(2)}, u32[]{:S(2)}) collective-permute-start(bf16[16,2,3072]{2,1,0:T(2,128)(2,1)S(1)} %collective-permute-done.3), channel_id=1, source_target_pairs={{0,30},{2,0},{4,2},{6,4},{8,6},{10,8},{12,10},{14,12},{16,14},{18,... | collective-permute-start | bytes 589832 | tf_op jit(solution)/shard_map/ppermute | solution.py:24
  40.7 0.2 constant_dynamic-update-slice_fusion.12
  40.9 0.2 constant_dynamic-update-slice_fusion.11
  41.0 4.0 %collective-permute-done.4 = bf16[16,2,3072]{2,1,0:T(2,128)(2,1)S(1)} collective-permute-done((bf16[16,2,3072]{2,1,0:T(2,128)(2,1)S(1)}, bf16[16,2,3072]{2,1,0:T(2,128)(2,1)S(1)}, u32[]{:S(2)}, u32[]{:S(2)}) %collective-permute-start.4) | collective-permute-done | bytes 196640 | tf_op jit(solution)/shard_map/ppermute | solution.py:21
  45.0 0.7 collective-permute-done.5
  45.7 5.1 %collective-permute-start.7 = (bf16[16,2,3072]{2,1,0:T(2,128)(2,1)S(1)}, bf16[16,2,3072]{2,1,0:T(2,128)(2,1)S(1)}, u32[]{:S(2)}, u32[]{:S(2)}) collective-permute-start(bf16[16,2,3072]{2,1,0:T(2,128)(2,1)S(1)} %collective-permute-done.5), channel_id=1, source_target_pairs={{0,30},{2,0},{4,2},{6,4},{8,6},{10,8},{12,10},{14,12},{16,14},{18,... | collective-permute-start | bytes 589832 | tf_op jit(solution)/shard_map/ppermute | solution.py:24
  50.8 0.2 constant_dynamic-update-slice_fusion.10
  51.0 0.2 constant_dynamic-update-slice_fusion.9
  51.1 3.3 collective-permute-done.6
  54.5 5.3 %collective-permute-start.9 = (bf16[16,2,3072]{2,1,0:T(2,128)(2,1)S(1)}, bf16[16,2,3072]{2,1,0:T(2,128)(2,1)S(1)}, u32[]{:S(2)}, u32[]{:S(2)}) collective-permute-start(bf16[16,2,3072]{2,1,0:T(2,128)(2,1)S(1)} %collective-permute-done.7), channel_id=1, source_target_pairs={{0,30},{2,0},{4,2},{6,4},{8,6},{10,8},{12,10},{14,12},{16,14},{18,... | collective-permute-start | bytes 589832 | tf_op jit(solution)/shard_map/ppermute | solution.py:24
  59.8 0.2 constant_dynamic-update-slice_fusion.8
  60.0 0.2 constant_dynamic-update-slice_fusion.7
  60.1 8.0 %collective-permute-done.8 = bf16[16,2,3072]{2,1,0:T(2,128)(2,1)S(1)} collective-permute-done((bf16[16,2,3072]{2,1,0:T(2,128)(2,1)S(1)}, bf16[16,2,3072]{2,1,0:T(2,128)(2,1)S(1)}, u32[]{:S(2)}, u32[]{:S(2)}) %collective-permute-start.8) | collective-permute-done | bytes 196640 | tf_op jit(solution)/shard_map/ppermute | solution.py:21
  68.2 5.4 %collective-permute-start.11 = (bf16[16,2,3072]{2,1,0:T(2,128)(2,1)S(1)}, bf16[16,2,3072]{2,1,0:T(2,128)(2,1)S(1)}, u32[]{:S(2)}, u32[]{:S(2)}) collective-permute-start(bf16[16,2,3072]{2,1,0:T(2,128)(2,1)S(1)} %collective-permute-done.9), channel_id=1, source_target_pairs={{0,30},{2,0},{4,2},{6,4},{8,6},{10,8},{12,10},{14,12},{16,14},{18,... | collective-permute-start | bytes 589832 | tf_op jit(solution)/shard_map/ppermute | solution.py:24
  73.6 0.2 constant_dynamic-update-slice_fusion.6
  73.7 0.2 constant_dynamic-update-slice_fusion.5
  73.9 6.7 %collective-permute-done.10 = bf16[16,2,3072]{2,1,0:T(2,128)(2,1)S(1)} collective-permute-done((bf16[16,2,3072]{2,1,0:T(2,128)(2,1)S(1)}, bf16[16,2,3072]{2,1,0:T(2,128)(2,1)S(1)}, u32[]{:S(2)}, u32[]{:S(2)}) %collective-permute-start.10) | collective-permute-done | bytes 196640 | tf_op jit(solution)/shard_map/ppermute | solution.py:21
  80.6 5.7 %collective-permute-start.13 = (bf16[16,2,3072]{2,1,0:T(2,128)(2,1)S(1)}, bf16[16,2,3072]{2,1,0:T(2,128)(2,1)S(1)}, u32[]{:S(2)}, u32[]{:S(2)}) collective-permute-start(bf16[16,2,3072]{2,1,0:T(2,128)(2,1)S(1)} %collective-permute-done.11), channel_id=1, source_target_pairs={{0,30},{2,0},{4,2},{6,4},{8,6},{10,8},{12,10},{14,12},{16,14},{18,... | collective-permute-start | bytes 589832 | tf_op jit(solution)/shard_map/ppermute | solution.py:24
  86.2 0.2 constant_dynamic-update-slice_fusion.4
  86.4 0.2 constant_dynamic-update-slice_fusion.3
  86.6 5.3 %collective-permute-done.12 = bf16[16,2,3072]{2,1,0:T(2,128)(2,1)S(1)} collective-permute-done((bf16[16,2,3072]{2,1,0:T(2,128)(2,1)S(1)}, bf16[16,2,3072]{2,1,0:T(2,128)(2,1)S(1)}, u32[]{:S(2)}, u32[]{:S(2)}) %collective-permute-start.12) | collective-permute-done | bytes 196640 | tf_op jit(solution)/shard_map/ppermute | solution.py:21
  91.9 0.2 constant_dynamic-update-slice_fusion.2
  92.1 0.2 constant_dynamic-update-slice_fusion.1
  92.2 8.4 %collective-permute-done.14 = bf16[16,2,3072]{2,1,0:T(2,128)(2,1)S(1)} collective-permute-done((bf16[16,2,3072]{2,1,0:T(2,128)(2,1)S(1)}, bf16[16,2,3072]{2,1,0:T(2,128)(2,1)S(1)}, u32[]{:S(2)}, u32[]{:S(2)}) %collective-permute-start.14) | collective-permute-done | bytes 196640 | tf_op jit(solution)/shard_map/ppermute | solution.py:21
  100.6 0.2 constant_dynamic-update-slice_fusion
  100.8 2.7 reshape.60
  103.5 7.0 %fusion.44 = f32[512,768]{1,0:T(8,128)} fusion(bf16[512,3072]{1,0:T(8,128)(2,1)} %reshape.60, bf16[3072,768]{1,0:T(8,128)(2,1)} %param.9), kind=kOutput, calls=%fused_computation.83 | convolution fusion | flops 2415919104 | bytes 9437184 | tf_op jit(solution)/shard_map/dot_general | solution.py:78
  110.5 6.3 %reshape.59 = bf16[512,3072]{1,0:T(8,128)(2,1)S(1)} reshape(bf16[256,2,3072]{2,1,0:T(2,128)(2,1)} %all-gather.2.cloned.1.call-done) | data formatting | bytes 6291456 | tf_op jit(solution)/shard_map/reshape | solution.py:77
  116.9 6.2 %fusion.43 = f32[512,768]{1,0:T(8,128)} fusion(bf16[512,3072]{1,0:T(8,128)(2,1)S(1)} %reshape.59, bf16[768,3072]{1,0:T(8,128)(2,1)} %param.10), kind=kOutput, calls=%fused_computation.82 | convolution fusion | flops 2415919104 | bytes 9437184 | tf_op jit(solution)/shard_map/td,hd->th/dot_general | solution.py:79
  123.0 0.0 all-reduce.7.cloned.1.call-update
  123.1 0.3 reduce-scatter.2.cloned.1.call-start
  123.3 35.1 %all-reduce.7.cloned.1.call-done = (f32[512,768]{1,0:T(8,128)}, f32[512,768]{1,0:T(8,128)}) async-done(((f32[512,768]{1,0:T(8,128)}, f32[512,768]{1,0:T(8,128)}), (f32[512,768]{1,0:T(8,128)}, f32[512,768]{1,0:T(8,128)})) %all-reduce.7.cloned.1.call-update) | async-done | bytes 3145744 | tf_op jit(solution)/shard_map/psum | solution.py:82
  158.5 9.2 %fusion.8 = f32[512,3072]{1,0:T(8,128)} fusion(bf16[3072,768]{1,0:T(8,128)(2,1)} %param.9, f32[512,768]{1,0:T(8,128)} %get-tuple-element.7, f32[512,768]{1,0:T(8,128)} %get-tuple-element.8), kind=kOutput, calls=%fused_computation.12 | convolution fusion | flops 2423390208 | bytes 14155776 | tf_op jit(solution)/shard_map/th,dh->td/dot_general | solution.py:85
  167.7 0.0 reduce-scatter.2.cloned.1.call-update
  167.8 0.0 all-reduce.5.cloned.1.call-start
  167.8 87.5 %reduce-scatter.2.cloned.1.call-done = f32[32,3072]{1,0:T(8,128)} async-done(((f32[512,3072]{1,0:T(8,128)}), f32[32,3072]{1,0:T(8,128)}) %reduce-scatter.2.cloned.1.call-update) | async-done | bytes 393232 | tf_op jit(solution)/shard_map/reduce_scatter | solution.py:84
  255.3 1.2 reshape.61
  256.5 0.5 multiply_reduce_fusion
  257.0 1.1 multiply_reduce_fusion.1
  258.1 0.1 reduce_sum.50
  258.2 3.3 all-reduce
  261.5 2.3 convolution_bitcast_fusion
  263.9 0.1 convert_reduce_fusion
  264.0 74.5 %all-reduce.5.cloned.1.call-done = f32[16,4,3072]{2,1,0:T(4,128)} async-done(((f32[16,4,3072]{2,1,0:T(4,128)}), f32[16,4,3072]{2,1,0:T(4,128)}) %all-reduce.5.cloned.1.call-update) | async-done | bytes 786448 | tf_op jit(solution)/shard_map/psum | solution.py:101
  338.4 2.3 broadcast_divide_fusion
  (38 shorter events, 0.1 us)
Async XLA Ops:
  6.5 1.5 copy-start
  6.5 104.0 %all-gather.2.cloned.1.call-start = ((), (), s32[]{:S(2)}) async-start(), calls=%async_computation.1 | async-start | bytes 3342336 | tf_op jit(solution)/shard_map/all_gather | solution.py:74
  8.1 6.2 %copy-start.7 = (s32[2]{0:T(128)}, s32[2]{0:T(128)S(1)}, u32[]{:S(2)}) copy-start(s32[2]{0:T(128)S(1)} %fusion.34) | copy-start | bytes 28
  9.0 5.3 %copy-start.1 = (f32[16,2,3072]{2,1,0:T(2,128)}, f32[16,2,3072]{2,1,0:T(2,128)S(1)}, u32[]{:S(2)}) copy-start(f32[16,2,3072]{2,1,0:T(2,128)S(1)} %get-tuple-element.12) | copy-start | bytes 1179652
  14.3 1.6 copy-start.2
  17.7 7.8 %collective-permute-start = (bf16[16,2,3072]{2,1,0:T(2,128)(2,1)}, bf16[16,2,3072]{2,1,0:T(2,128)(2,1)}, u32[]{:S(2)}, u32[]{:S(2)}) collective-permute-start(bf16[16,2,3072]{2,1,0:T(2,128)(2,1)} %get-tuple-element.10), channel_id=1, source_target_pairs={{0,2},{2,4},{4,6},{6,8},{8,10},{10,12},{12,14},{14,16},{16,18},{18... | collective-permute-start | bytes 589832 | tf_op jit(solution)/shard_map/ppermute | solution.py:21
  19.2 7.3 %collective-permute-start.1 = (bf16[16,2,3072]{2,1,0:T(2,128)(2,1)}, bf16[16,2,3072]{2,1,0:T(2,128)(2,1)}, u32[]{:S(2)}, u32[]{:S(2)}) collective-permute-start(bf16[16,2,3072]{2,1,0:T(2,128)(2,1)} %get-tuple-element.10), channel_id=1, source_target_pairs={{0,30},{2,0},{4,2},{6,4},{8,6},{10,8},{12,10},{14,12},{16,14},{18,... | collective-permute-start | bytes 589832 | tf_op jit(solution)/shard_map/ppermute | solution.py:24
  20.0 138.5 %all-reduce.7.cloned.1.call-start = ((), (), s32[]{:S(2)}) async-start(), calls=%async_computation.4 | async-start | bytes 6291456 | tf_op jit(solution)/shard_map/psum | solution.py:82
  25.5 9.7 %collective-permute-start.2 = (bf16[16,2,3072]{2,1,0:T(2,128)(2,1)}, bf16[16,2,3072]{2,1,0:T(2,128)(2,1)S(1)}, u32[]{:S(2)}, u32[]{:S(2)}) collective-permute-start(bf16[16,2,3072]{2,1,0:T(2,128)(2,1)} %collective-permute-done), channel_id=1, source_target_pairs={{0,2},{2,4},{4,6},{6,8},{8,10},{10,12},{12,14},{14,16},{16,18},{18... | collective-permute-start | bytes 589832 | tf_op jit(solution)/shard_map/ppermute | solution.py:21
  26.5 8.7 %collective-permute-start.3 = (bf16[16,2,3072]{2,1,0:T(2,128)(2,1)}, bf16[16,2,3072]{2,1,0:T(2,128)(2,1)S(1)}, u32[]{:S(2)}, u32[]{:S(2)}) collective-permute-start(bf16[16,2,3072]{2,1,0:T(2,128)(2,1)} %collective-permute-done.1), channel_id=1, source_target_pairs={{0,30},{2,0},{4,2},{6,4},{8,6},{10,8},{12,10},{14,12},{16,14},{18,... | collective-permute-start | bytes 589832 | tf_op jit(solution)/shard_map/ppermute | solution.py:24
  35.2 9.8 %collective-permute-start.4 = (bf16[16,2,3072]{2,1,0:T(2,128)(2,1)S(1)}, bf16[16,2,3072]{2,1,0:T(2,128)(2,1)S(1)}, u32[]{:S(2)}, u32[]{:S(2)}) collective-permute-start(bf16[16,2,3072]{2,1,0:T(2,128)(2,1)S(1)} %collective-permute-done.2), channel_id=1, source_target_pairs={{0,2},{2,4},{4,6},{6,8},{8,10},{10,12},{12,14},{14,16},{16,18},{18... | collective-permute-start | bytes 589832 | tf_op jit(solution)/shard_map/ppermute | solution.py:21
  35.2 10.5 %collective-permute-start.5 = (bf16[16,2,3072]{2,1,0:T(2,128)(2,1)S(1)}, bf16[16,2,3072]{2,1,0:T(2,128)(2,1)S(1)}, u32[]{:S(2)}, u32[]{:S(2)}) collective-permute-start(bf16[16,2,3072]{2,1,0:T(2,128)(2,1)S(1)} %collective-permute-done.3), channel_id=1, source_target_pairs={{0,30},{2,0},{4,2},{6,4},{8,6},{10,8},{12,10},{14,12},{16,14},{18,... | collective-permute-start | bytes 589832 | tf_op jit(solution)/shard_map/ppermute | solution.py:24
  45.0 9.4 %collective-permute-start.6 = (bf16[16,2,3072]{2,1,0:T(2,128)(2,1)S(1)}, bf16[16,2,3072]{2,1,0:T(2,128)(2,1)S(1)}, u32[]{:S(2)}, u32[]{:S(2)}) collective-permute-start(bf16[16,2,3072]{2,1,0:T(2,128)(2,1)S(1)} %collective-permute-done.4), channel_id=1, source_target_pairs={{0,2},{2,4},{4,6},{6,8},{8,10},{10,12},{12,14},{14,16},{16,18},{18... | collective-permute-start | bytes 589832 | tf_op jit(solution)/shard_map/ppermute | solution.py:21
  45.7 8.7 %collective-permute-start.7 = (bf16[16,2,3072]{2,1,0:T(2,128)(2,1)S(1)}, bf16[16,2,3072]{2,1,0:T(2,128)(2,1)S(1)}, u32[]{:S(2)}, u32[]{:S(2)}) collective-permute-start(bf16[16,2,3072]{2,1,0:T(2,128)(2,1)S(1)} %collective-permute-done.5), channel_id=1, source_target_pairs={{0,30},{2,0},{4,2},{6,4},{8,6},{10,8},{12,10},{14,12},{16,14},{18,... | collective-permute-start | bytes 589832 | tf_op jit(solution)/shard_map/ppermute | solution.py:24
  54.5 13.7 %collective-permute-start.8 = (bf16[16,2,3072]{2,1,0:T(2,128)(2,1)S(1)}, bf16[16,2,3072]{2,1,0:T(2,128)(2,1)S(1)}, u32[]{:S(2)}, u32[]{:S(2)}) collective-permute-start(bf16[16,2,3072]{2,1,0:T(2,128)(2,1)S(1)} %collective-permute-done.6), channel_id=1, source_target_pairs={{0,2},{2,4},{4,6},{6,8},{8,10},{10,12},{12,14},{14,16},{16,18},{18... | collective-permute-start | bytes 589832 | tf_op jit(solution)/shard_map/ppermute | solution.py:21
  54.5 13.7 %collective-permute-start.9 = (bf16[16,2,3072]{2,1,0:T(2,128)(2,1)S(1)}, bf16[16,2,3072]{2,1,0:T(2,128)(2,1)S(1)}, u32[]{:S(2)}, u32[]{:S(2)}) collective-permute-start(bf16[16,2,3072]{2,1,0:T(2,128)(2,1)S(1)} %collective-permute-done.7), channel_id=1, source_target_pairs={{0,30},{2,0},{4,2},{6,4},{8,6},{10,8},{12,10},{14,12},{16,14},{18,... | collective-permute-start | bytes 589832 | tf_op jit(solution)/shard_map/ppermute | solution.py:24
  68.2 12.4 %collective-permute-start.10 = (bf16[16,2,3072]{2,1,0:T(2,128)(2,1)S(1)}, bf16[16,2,3072]{2,1,0:T(2,128)(2,1)S(1)}, u32[]{:S(2)}, u32[]{:S(2)}) collective-permute-start(bf16[16,2,3072]{2,1,0:T(2,128)(2,1)S(1)} %collective-permute-done.8), channel_id=1, source_target_pairs={{0,2},{2,4},{4,6},{6,8},{8,10},{10,12},{12,14},{14,16},{16,18},{18... | collective-permute-start | bytes 589832 | tf_op jit(solution)/shard_map/ppermute | solution.py:21
  68.2 12.4 %collective-permute-start.11 = (bf16[16,2,3072]{2,1,0:T(2,128)(2,1)S(1)}, bf16[16,2,3072]{2,1,0:T(2,128)(2,1)S(1)}, u32[]{:S(2)}, u32[]{:S(2)}) collective-permute-start(bf16[16,2,3072]{2,1,0:T(2,128)(2,1)S(1)} %collective-permute-done.9), channel_id=1, source_target_pairs={{0,30},{2,0},{4,2},{6,4},{8,6},{10,8},{12,10},{14,12},{16,14},{18,... | collective-permute-start | bytes 589832 | tf_op jit(solution)/shard_map/ppermute | solution.py:24
  80.6 11.3 %collective-permute-start.12 = (bf16[16,2,3072]{2,1,0:T(2,128)(2,1)S(1)}, bf16[16,2,3072]{2,1,0:T(2,128)(2,1)S(1)}, u32[]{:S(2)}, u32[]{:S(2)}) collective-permute-start(bf16[16,2,3072]{2,1,0:T(2,128)(2,1)S(1)} %collective-permute-done.10), channel_id=1, source_target_pairs={{0,2},{2,4},{4,6},{6,8},{8,10},{10,12},{12,14},{14,16},{16,18},{18... | collective-permute-start | bytes 589832 | tf_op jit(solution)/shard_map/ppermute | solution.py:21
  80.6 11.5 %collective-permute-start.13 = (bf16[16,2,3072]{2,1,0:T(2,128)(2,1)S(1)}, bf16[16,2,3072]{2,1,0:T(2,128)(2,1)S(1)}, u32[]{:S(2)}, u32[]{:S(2)}) collective-permute-start(bf16[16,2,3072]{2,1,0:T(2,128)(2,1)S(1)} %collective-permute-done.11), channel_id=1, source_target_pairs={{0,30},{2,0},{4,2},{6,4},{8,6},{10,8},{12,10},{14,12},{16,14},{18,... | collective-permute-start | bytes 589832 | tf_op jit(solution)/shard_map/ppermute | solution.py:24
  91.9 8.7 %collective-permute-start.14 = (bf16[16,2,3072]{2,1,0:T(2,128)(2,1)S(1)}, bf16[16,2,3072]{2,1,0:T(2,128)(2,1)S(1)}, u32[]{:S(2)}, u32[]{:S(2)}) collective-permute-start(bf16[16,2,3072]{2,1,0:T(2,128)(2,1)S(1)} %collective-permute-done.12), channel_id=1, source_target_pairs={{0,2},{2,4},{4,6},{6,8},{8,10},{10,12},{12,14},{14,16},{16,18},{18... | collective-permute-start | bytes 589832 | tf_op jit(solution)/shard_map/ppermute | solution.py:21
  123.1 132.2 %reduce-scatter.2.cloned.1.call-start = ((), (), s32[]{:S(2)}) async-start(), calls=%async_computation.2 | async-start | bytes 6684672 | tf_op jit(solution)/shard_map/reduce_scatter | solution.py:84
  167.7 88.8 %copy-start.3 = (f32[16,2,3072]{2,1,0:T(2,128)S(1)}, f32[16,2,3072]{2,1,0:T(2,128)}, u32[]{:S(2)}) copy-start(f32[16,2,3072]{2,1,0:T(2,128)} %copy-done.1) | copy-start | bytes 1179652
  167.7 88.8 %copy-start.5 = (f32[3072]{0:T(1024)S(1)}, f32[3072]{0:T(1024)}, u32[]{:S(2)}) copy-start(f32[3072]{0:T(1024)} %param.8) | copy-start | bytes 36868
  167.7 93.8 %copy-start.4 = (bf16[16,2,3072]{2,1,0:T(2,128)(2,1)S(1)}, bf16[16,2,3072]{2,1,0:T(2,128)(2,1)}, u32[]{:S(2)}) copy-start(bf16[16,2,3072]{2,1,0:T(2,128)(2,1)} %param.11) | copy-start | bytes 589828
  167.7 93.8 %copy-start.8 = (s32[2]{0:T(128)S(1)}, s32[2]{0:T(128)}, u32[]{:S(2)}) copy-start(s32[2]{0:T(128)} %copy-done.7) | copy-start | bytes 28
  167.7 96.1 %copy-start.6 = (s32[16,1]{0,1:T(1,128)S(1)}, s32[16,1]{0,1:T(1,128)}, u32[]{:S(2)}) copy-start(s32[16,1]{0,1:T(1,128)} %param.13) | copy-start | bytes 196
  167.8 170.7 %all-reduce.5.cloned.1.call-start = ((), (), s32[]{:S(2)}) async-start(), calls=%async_computation.3 | async-start | bytes 1572864 | tf_op jit(solution)/shard_map/psum | solution.py:101
Sparse Core Ops, SparseCore 0:
  20.1 61.2 all-gather.1
  123.2 35.2 all-reduce.6
  167.9 87.3 reduce-scatter.1
  264.0 74.4 all-reduce.4
